TPU v7x, 32 devices: a whole 2x2x4 slice. The times are simulated.
32 devices in a mesh: section: 8 (over y, x, core), dp: 4 (over z).
Axes of the slice: x: 2, y: 2, z: 4, core: 2. Of those that a mesh axis runs over, the one named last changes fastest.
Arguments:
- images: bfloat16 [12, 256, 512], P(None, 'dp'), may hold values from -6 to 6
- cotangent: bfloat16 [12, 256, 512], P(None, 'dp'), may hold values from -6 to 6
- w_in: bfloat16 [8, 4, 512, 512], P('section', None, 'dp'), may hold values from -0.25 to 0.25
- w_out: bfloat16 [8, 4, 512, 512], P('section', None, 'dp'), may hold values from -0.0625 to 0.0625
Outputs:
- new_in: float32 [8, 4, 512, 512], P('section', None, 'dp')
- new_out: float32 [8, 4, 512, 512], P('section', None, 'dp')
All inputs are finite; a program needn't handle non-finite values.
Results may differ from a plain program's by a relative error of at most 0.03.
Values may be sent and summed in bfloat16 or wider, within the bound.
A program may use at most 128 MiB of HBM per device.

v0:
```python
import math
import jax
import jax.numpy as jnp
from jax import lax
from jax.sharding import PartitionSpec as P


def shifted(value, axis, steps):
    count = lax.axis_size(axis)
    initial, last = (max(0, -steps), min(count, count - steps))
    return lax.ppermute(value, axis, [(source, source + steps) for source in range(initial, last)])


def per_device(images, cotangent, w_in, w_out):
    sections = lax.axis_size("section")
    place = lax.axis_index("section")
    groups = lax.axis_size("dp")
    full_in, full_out = (
        lax.all_gather(w_in, "dp", axis=2, tiled=True),
        lax.all_gather(w_out, "dp", axis=2, tiled=True),
    )
    first = full_in[0]
    second = full_out[0]
    micro, rows, width = images.shape
    layers = first.shape[0]
    ticks = micro + sections - 1
    zero_rows = jnp.zeros((rows, width), jnp.bfloat16)
    zero_stack = jnp.zeros((layers, rows, width), jnp.bfloat16)
    contract = (((1,), (1,)), ((), ()))

    def forward_section(value):
        inputs = []
        for layer in range(layers):
            inputs.append(value)
            pre = jnp.dot(value, first[layer], preferred_element_type=jnp.float32)
            hidden = (pre * jax.nn.sigmoid(pre)).astype(jnp.bfloat16)
            value = (
                value.astype(jnp.float32)
                + jnp.dot(hidden, second[layer], preferred_element_type=jnp.float32)
            ).astype(jnp.bfloat16)
        return (value, jnp.stack(inputs))

    def backward_section(inputs, grad):
        hiddens, dpres, grads = ([], [], [])
        for layer in reversed(range(layers)):
            value = inputs[layer]
            pre = jnp.dot(value, first[layer], preferred_element_type=jnp.float32)
            sig = jax.nn.sigmoid(pre)
            hiddens.append((pre * sig).astype(jnp.bfloat16))
            grads.append(grad)
            dhidden = lax.dot_general(
                grad, second[layer], contract, preferred_element_type=jnp.float32
            )
            dpre = (dhidden * (sig * (1.0 + pre * (1.0 - sig)))).astype(jnp.bfloat16)
            dpres.append(dpre)
            grad = (
                grad.astype(jnp.float32)
                + lax.dot_general(dpre, first[layer], contract, preferred_element_type=jnp.float32)
            ).astype(jnp.bfloat16)
        return (grad, jnp.stack(hiddens[::-1]), jnp.stack(dpres[::-1]), jnp.stack(grads[::-1]))

    def put(store, index, valid, fresh, axis_pos):
        old = lax.dynamic_index_in_dim(store, index, axis_pos, keepdims=False)
        return lax.dynamic_update_index_in_dim(store, jnp.where(valid, fresh, old), index, axis_pos)

    kept0 = jnp.zeros((layers, micro, rows, width), jnp.bfloat16)

    def forward_tick(carry, tick):
        incoming, kept = carry
        slot = tick - place
        valid = (slot >= 0) & (slot < micro)
        index = jnp.clip(slot, 0, micro - 1)
        fresh = lax.dynamic_index_in_dim(images, index, 0, keepdims=False)
        source = jnp.where(place == 0, fresh, incoming)
        output, inputs = lax.cond(
            valid, lambda: forward_section(source), lambda: (zero_rows, zero_stack)
        )
        kept = put(kept, index, valid, inputs, 1)
        passed = shifted(output, "section", 1)
        return ((passed, kept), None)

    (unused_in, kept), unused = lax.scan(
        forward_tick, (zero_rows, kept0), jnp.arange(ticks, dtype=jnp.int32)
    )

    def relay_step(tick, incoming):
        slot = tick - (sections - 1 - place)
        valid = (slot >= 0) & (slot < micro)
        index = jnp.clip(slot, 0, micro - 1)
        fresh = lax.dynamic_index_in_dim(cotangent, index, 0, keepdims=False)
        upstream = jnp.where(place == sections - 1, fresh, incoming)
        inputs = lax.dynamic_index_in_dim(kept, index, 1, keepdims=False)

        def run():
            back, hiddens, dpres, grads = backward_section(inputs, upstream)
            return (back, hiddens, dpres, grads)

        back, hiddens, dpres, grads = lax.cond(
            valid, run, lambda: (zero_rows, zero_stack, zero_stack, zero_stack)
        )
        passed = shifted(back, "section", -1)
        return (passed, valid, index, inputs, hiddens, dpres, grads)

    blank = jnp.zeros((layers, micro, rows, width), jnp.bfloat16)

    def backward_tick(carry, tick):
        incoming, hidden_all, dpre_all, grad_all = carry
        passed, valid, index, inputs, hiddens, dpres, grads = relay_step(tick, incoming)
        hidden_all = put(hidden_all, index, valid, hiddens, 1)
        dpre_all = put(dpre_all, index, valid, dpres, 1)
        grad_all = put(grad_all, index, valid, grads, 1)
        return ((passed, hidden_all, dpre_all, grad_all), None)

    (unused_back, hidden_all, dpre_all, grad_all), unused = lax.scan(
        backward_tick, (zero_rows, blank, blank, blank), jnp.arange(ticks, dtype=jnp.int32)
    )
    flat_inputs = kept.reshape(layers, micro * rows, width)
    flat_hidden = hidden_all.reshape(layers, micro * rows, width)
    flat_dpre = dpre_all.reshape(layers, micro * rows, width)
    flat_grad = grad_all.reshape(layers, micro * rows, width)
    grad_in = None
    grad_out = None
    grad_in = jnp.einsum("lrc,lrd->lcd", flat_inputs, flat_dpre, preferred_element_type=jnp.float32)
    grad_out = jnp.einsum(
        "lrc,lrd->lcd", flat_hidden, flat_grad, preferred_element_type=jnp.float32
    )
    share_in, share_out = (
        lax.psum_scatter(grad_in, "dp", scatter_dimension=1, tiled=True),
        lax.psum_scatter(grad_out, "dp", scatter_dimension=1, tiled=True),
    )
    rate = 0.1 / math.sqrt(micro * rows * groups)
    new_in = w_in.astype(jnp.float32) - rate * share_in[None]
    new_out = w_out.astype(jnp.float32) - rate * share_out[None]
    return (new_in, new_out)


def solution(mesh):
    in_specs = (
        P(None, "dp", None),
        P(None, "dp", None),
        P("section", None, "dp", None),
        P("section", None, "dp", None),
    )
    out_specs = (P("section", None, "dp", None), P("section", None, "dp", None))
    return jax.shard_map(
        per_device, mesh=mesh, in_specs=in_specs, out_specs=out_specs, check_vma=False
    )
```

profile of v0, /device:TPU:0, one launch (start us, length us, event | category | flops | bytes accessed | tf_op | source)
XLA Modules:
  0.0 829.8 jit_solution(466928142596177172)
XLA Ops:
  8.7 49.5 %all-gather.3.cloned.1.call-done = bf16[1,4,512,512]{3,2,1,0:T(8,128)(2,1)} async-done(((bf16[1,4,128,512]{3,2,1,0:T(8,128)(2,1)}), bf16[1,4,512,512]{3,2,1,0:T(8,128)(2,1)}) %all-gather.3.cloned.1.call-update) | async-done | bytes 2097168 | tf_op jit(solution)/shard_map/all_gather | solution.py:19
  58.2 46.3 %all-gather.5.cloned.1.call-done = bf16[1,4,512,512]{3,2,1,0:T(8,128)(2,1)} async-done(((bf16[1,4,128,512]{3,2,1,0:T(8,128)(2,1)}), bf16[1,4,512,512]{3,2,1,0:T(8,128)(2,1)}) %all-gather.5.cloned.1.call-update) | async-done | bytes 2097168 | tf_op jit(solution)/shard_map/all_gather | solution.py:20
  106.5 235.0 %while.31 = (s32[]{:T(128)}, bf16[64,512]{1,0:T(8,128)(2,1)S(1)}, bf16[4,12,64,512]{3,2,1,0:T(8,128)(2,1)}, s32[19]{0:T(128)S(1)}, s32[]{:T(128)}, /*index=5*/pr...) while((s32[]{:T(128)}, bf16[64,512]{1,0:T(8,128)(2,1)S(1)}, ...), condition=%wide.region_3.4_spmd, body=%wide.region_0.3_spmd.sunk | while | flops 270106624 | bytes 7408441 | solution.py:82
  107.8 6.7 conditional.4
  118.8 6.7 conditional.4
  129.9 6.7 conditional.4
  141.5 6.7 conditional.4
  148.2 3.8 collective-permute-start
  155.1 6.7 conditional.4
  168.6 6.7 conditional.4
  175.3 3.9 collective-permute-start
  182.2 6.7 conditional.4
  188.8 3.8 collective-permute-start
  195.7 6.7 conditional.4
  202.4 3.8 collective-permute-start
  209.2 6.7 conditional.4
  215.9 3.9 collective-permute-start
  222.8 6.7 conditional.4
  229.5 3.8 collective-permute-start
  236.3 6.7 conditional.4
  243.0 3.8 collective-permute-start
  249.9 6.7 conditional.4
  256.5 3.8 collective-permute-start
  263.4 10.5 %collective-permute-start = (bf16[64,512]{1,0:T(8,128)(2,1)S(1)}, bf16[64,512]{1,0:T(8,128)(2,1)S(1)}, u32[]{:S(2)}, u32[]{:S(2)}) collective-permute-start(bf16[64,512]{1,0:T(8,128)(2,1)S(1)} %get-tuple-element.520), channel_id=1, source_target_pairs={{0,4},{4,8},{8,12},{12,16},{16,20},{20,24},{24,28},{1,5},{5,9},{9,... | collective-permute-start | bytes 196616 | tf_op jit(solution)/shard_map/while/body/eval_jaxpr/ppermute | solution.py:11
  277.0 3.8 collective-permute-start
  283.9 11.3 %collective-permute-start = (bf16[64,512]{1,0:T(8,128)(2,1)S(1)}, bf16[64,512]{1,0:T(8,128)(2,1)S(1)}, u32[]{:S(2)}, u32[]{:S(2)}) collective-permute-start(bf16[64,512]{1,0:T(8,128)(2,1)S(1)} %get-tuple-element.520), channel_id=1, source_target_pairs={{0,4},{4,8},{8,12},{12,16},{16,20},{20,24},{24,28},{1,5},{5,9},{9,... | collective-permute-start | bytes 196616 | tf_op jit(solution)/shard_map/while/body/eval_jaxpr/ppermute | solution.py:11
  298.4 4.7 collective-permute-start
  306.2 11.3 %collective-permute-start = (bf16[64,512]{1,0:T(8,128)(2,1)S(1)}, bf16[64,512]{1,0:T(8,128)(2,1)S(1)}, u32[]{:S(2)}, u32[]{:S(2)}) collective-permute-start(bf16[64,512]{1,0:T(8,128)(2,1)S(1)} %get-tuple-element.520), channel_id=1, source_target_pairs={{0,4},{4,8},{8,12},{12,16},{16,20},{20,24},{24,28},{1,5},{5,9},{9,... | collective-permute-start | bytes 196616 | tf_op jit(solution)/shard_map/while/body/eval_jaxpr/ppermute | solution.py:11
  320.6 4.7 collective-permute-start
  328.5 11.3 %collective-permute-start = (bf16[64,512]{1,0:T(8,128)(2,1)S(1)}, bf16[64,512]{1,0:T(8,128)(2,1)S(1)}, u32[]{:S(2)}, u32[]{:S(2)}) collective-permute-start(bf16[64,512]{1,0:T(8,128)(2,1)S(1)} %get-tuple-element.520), channel_id=1, source_target_pairs={{0,4},{4,8},{8,12},{12,16},{16,20},{20,24},{24,28},{1,5},{5,9},{9,... | collective-permute-start | bytes 196616 | tf_op jit(solution)/shard_map/while/body/eval_jaxpr/ppermute | solution.py:11
  347.8 312.3 %while.32 = (s32[]{:T(128)}, bf16[64,512]{1,0:T(8,128)(2,1)S(1)}, bf16[4,12,64,512]{3,2,1,0:T(8,128)(2,1)}, bf16[4,12,64,512]{3,2,1,0:T(8,128)(2,1)}, bf16[4,12,...) while((s32[]{:T(128)}, bf16[64,512]{1,0:T(8,128)(2,1)S(1)}, ...), condition=%wide.region_7.8_spmd, body=%wide.region_4.7_spmd.sunk | while | flops 406487040 | bytes 24055228 | solution.py:114
  404.1 56.2 %collective-permute-done.1 = bf16[64,512]{1,0:T(8,128)(2,1)S(1)} collective-permute-done((bf16[64,512]{1,0:T(8,128)(2,1)S(1)}, bf16[64,512]{1,0:T(8,128)(2,1)S(1)}, u32[]{:S(2)}, u32[]{:S(2)}) %collective-permute-start.1) | collective-permute-done | bytes 65568 | tf_op jit(solution)/shard_map/while/body/eval_jaxpr/ppermute | solution.py:11
  461.5 8.9 %conditional.5 = (bf16[64,512]{1,0:T(8,128)(2,1)S(1)}, bf16[4,64,512]{2,1,0:T(8,128)(2,1)S(1)}, bf16[4,64,512]{2,1,0:T(8,128)(2,1)S(1)}, bf16[4,64,512]{2,1,0:T(8,128)(2,1)S(1)}) conditional(s32[]{:T(128)} %convert_element_type.194, () %tuple.83, (pred[]{:T(512)}, bf16[12,64,512]{2,1,0:T(8,128)(2,1)}, s32[]{:T(128)}, bf16[64,512]{1,0:T(8,128)(2,1)S(1)}, ...), branch_computations={%region_5.5_spmd, %region_6.6_spmd} | conditional | flops 406093824 | bytes 19859568 | solution.py:98
  478.2 8.9 %conditional.5 = (bf16[64,512]{1,0:T(8,128)(2,1)S(1)}, bf16[4,64,512]{2,1,0:T(8,128)(2,1)S(1)}, bf16[4,64,512]{2,1,0:T(8,128)(2,1)S(1)}, bf16[4,64,512]{2,1,0:T(8,128)(2,1)S(1)}) conditional(s32[]{:T(128)} %convert_element_type.194, () %tuple.83, (pred[]{:T(512)}, bf16[12,64,512]{2,1,0:T(8,128)(2,1)}, s32[]{:T(128)}, bf16[64,512]{1,0:T(8,128)(2,1)S(1)}, ...), branch_computations={%region_5.5_spmd, %region_6.6_spmd} | conditional | flops 406093824 | bytes 19859568 | solution.py:98
  494.9 8.9 %conditional.5 = (bf16[64,512]{1,0:T(8,128)(2,1)S(1)}, bf16[4,64,512]{2,1,0:T(8,128)(2,1)S(1)}, bf16[4,64,512]{2,1,0:T(8,128)(2,1)S(1)}, bf16[4,64,512]{2,1,0:T(8,128)(2,1)S(1)}) conditional(s32[]{:T(128)} %convert_element_type.194, () %tuple.83, (pred[]{:T(512)}, bf16[12,64,512]{2,1,0:T(8,128)(2,1)}, s32[]{:T(128)}, bf16[64,512]{1,0:T(8,128)(2,1)S(1)}, ...), branch_computations={%region_5.5_spmd, %region_6.6_spmd} | conditional | flops 406093824 | bytes 19859568 | solution.py:98
  511.6 8.9 %conditional.5 = (bf16[64,512]{1,0:T(8,128)(2,1)S(1)}, bf16[4,64,512]{2,1,0:T(8,128)(2,1)S(1)}, bf16[4,64,512]{2,1,0:T(8,128)(2,1)S(1)}, bf16[4,64,512]{2,1,0:T(8,128)(2,1)S(1)}) conditional(s32[]{:T(128)} %convert_element_type.194, () %tuple.83, (pred[]{:T(512)}, bf16[12,64,512]{2,1,0:T(8,128)(2,1)}, s32[]{:T(128)}, bf16[64,512]{1,0:T(8,128)(2,1)S(1)}, ...), branch_computations={%region_5.5_spmd, %region_6.6_spmd} | conditional | flops 406093824 | bytes 19859568 | solution.py:98
  528.3 8.9 %conditional.5 = (bf16[64,512]{1,0:T(8,128)(2,1)S(1)}, bf16[4,64,512]{2,1,0:T(8,128)(2,1)S(1)}, bf16[4,64,512]{2,1,0:T(8,128)(2,1)S(1)}, bf16[4,64,512]{2,1,0:T(8,128)(2,1)S(1)}) conditional(s32[]{:T(128)} %convert_element_type.194, () %tuple.83, (pred[]{:T(512)}, bf16[12,64,512]{2,1,0:T(8,128)(2,1)}, s32[]{:T(128)}, bf16[64,512]{1,0:T(8,128)(2,1)S(1)}, ...), branch_computations={%region_5.5_spmd, %region_6.6_spmd} | conditional | flops 406093824 | bytes 19859568 | solution.py:98
  545.0 8.9 %conditional.5 = (bf16[64,512]{1,0:T(8,128)(2,1)S(1)}, bf16[4,64,512]{2,1,0:T(8,128)(2,1)S(1)}, bf16[4,64,512]{2,1,0:T(8,128)(2,1)S(1)}, bf16[4,64,512]{2,1,0:T(8,128)(2,1)S(1)}) conditional(s32[]{:T(128)} %convert_element_type.194, () %tuple.83, (pred[]{:T(512)}, bf16[12,64,512]{2,1,0:T(8,128)(2,1)}, s32[]{:T(128)}, bf16[64,512]{1,0:T(8,128)(2,1)S(1)}, ...), branch_computations={%region_5.5_spmd, %region_6.6_spmd} | conditional | flops 406093824 | bytes 19859568 | solution.py:98
  561.7 8.9 %conditional.5 = (bf16[64,512]{1,0:T(8,128)(2,1)S(1)}, bf16[4,64,512]{2,1,0:T(8,128)(2,1)S(1)}, bf16[4,64,512]{2,1,0:T(8,128)(2,1)S(1)}, bf16[4,64,512]{2,1,0:T(8,128)(2,1)S(1)}) conditional(s32[]{:T(128)} %convert_element_type.194, () %tuple.83, (pred[]{:T(512)}, bf16[12,64,512]{2,1,0:T(8,128)(2,1)}, s32[]{:T(128)}, bf16[64,512]{1,0:T(8,128)(2,1)S(1)}, ...), branch_computations={%region_5.5_spmd, %region_6.6_spmd} | conditional | flops 406093824 | bytes 19859568 | solution.py:98
  578.4 8.9 %conditional.5 = (bf16[64,512]{1,0:T(8,128)(2,1)S(1)}, bf16[4,64,512]{2,1,0:T(8,128)(2,1)S(1)}, bf16[4,64,512]{2,1,0:T(8,128)(2,1)S(1)}, bf16[4,64,512]{2,1,0:T(8,128)(2,1)S(1)}) conditional(s32[]{:T(128)} %convert_element_type.194, () %tuple.83, (pred[]{:T(512)}, bf16[12,64,512]{2,1,0:T(8,128)(2,1)}, s32[]{:T(128)}, bf16[64,512]{1,0:T(8,128)(2,1)S(1)}, ...), branch_computations={%region_5.5_spmd, %region_6.6_spmd} | conditional | flops 406093824 | bytes 19859568 | solution.py:98
  595.1 8.9 %conditional.5 = (bf16[64,512]{1,0:T(8,128)(2,1)S(1)}, bf16[4,64,512]{2,1,0:T(8,128)(2,1)S(1)}, bf16[4,64,512]{2,1,0:T(8,128)(2,1)S(1)}, bf16[4,64,512]{2,1,0:T(8,128)(2,1)S(1)}) conditional(s32[]{:T(128)} %convert_element_type.194, () %tuple.83, (pred[]{:T(512)}, bf16[12,64,512]{2,1,0:T(8,128)(2,1)}, s32[]{:T(128)}, bf16[64,512]{1,0:T(8,128)(2,1)S(1)}, ...), branch_computations={%region_5.5_spmd, %region_6.6_spmd} | conditional | flops 406093824 | bytes 19859568 | solution.py:98
  611.9 8.9 %conditional.5 = (bf16[64,512]{1,0:T(8,128)(2,1)S(1)}, bf16[4,64,512]{2,1,0:T(8,128)(2,1)S(1)}, bf16[4,64,512]{2,1,0:T(8,128)(2,1)S(1)}, bf16[4,64,512]{2,1,0:T(8,128)(2,1)S(1)}) conditional(s32[]{:T(128)} %convert_element_type.194, () %tuple.83, (pred[]{:T(512)}, bf16[12,64,512]{2,1,0:T(8,128)(2,1)}, s32[]{:T(128)}, bf16[64,512]{1,0:T(8,128)(2,1)S(1)}, ...), branch_computations={%region_5.5_spmd, %region_6.6_spmd} | conditional | flops 406093824 | bytes 19859568 | solution.py:98
  628.5 8.9 %conditional.5 = (bf16[64,512]{1,0:T(8,128)(2,1)S(1)}, bf16[4,64,512]{2,1,0:T(8,128)(2,1)S(1)}, bf16[4,64,512]{2,1,0:T(8,128)(2,1)S(1)}, bf16[4,64,512]{2,1,0:T(8,128)(2,1)S(1)}) conditional(s32[]{:T(128)} %convert_element_type.194, () %tuple.83, (pred[]{:T(512)}, bf16[12,64,512]{2,1,0:T(8,128)(2,1)}, s32[]{:T(128)}, bf16[64,512]{1,0:T(8,128)(2,1)S(1)}, ...), branch_computations={%region_5.5_spmd, %region_6.6_spmd} | conditional | flops 406093824 | bytes 19859568 | solution.py:98
  645.2 8.9 %conditional.5 = (bf16[64,512]{1,0:T(8,128)(2,1)S(1)}, bf16[4,64,512]{2,1,0:T(8,128)(2,1)S(1)}, bf16[4,64,512]{2,1,0:T(8,128)(2,1)S(1)}, bf16[4,64,512]{2,1,0:T(8,128)(2,1)S(1)}) conditional(s32[]{:T(128)} %convert_element_type.194, () %tuple.83, (pred[]{:T(512)}, bf16[12,64,512]{2,1,0:T(8,128)(2,1)}, s32[]{:T(128)}, bf16[64,512]{1,0:T(8,128)(2,1)S(1)}, ...), branch_computations={%region_5.5_spmd, %region_6.6_spmd} | conditional | flops 406093824 | bytes 19859568 | solution.py:98
  660.1 6.6 fusion.96
  668.6 5.8 fusion.95
  674.4 66.9 %reduce-scatter.5.cloned.1.call-done = f32[4,128,512]{2,1,0:T(8,128)} async-done(((f32[4,512,512]{2,1,0:T(8,128)}), f32[4,128,512]{2,1,0:T(8,128)}) %reduce-scatter.5.cloned.1.call-update) | async-done | bytes 1048592 | tf_op jit(solution)/shard_map/reduce_scatter | solution.py:129
  743.7 77.2 %reduce-scatter.3.cloned.1.call-done = f32[4,128,512]{2,1,0:T(8,128)} async-done(((f32[4,512,512]{2,1,0:T(8,128)}), f32[4,128,512]{2,1,0:T(8,128)}) %reduce-scatter.3.cloned.1.call-update) | async-done | bytes 1048592 | tf_op jit(solution)/shard_map/reduce_scatter | solution.py:128
  (613 shorter events, 392.6 us)
Async XLA Ops:
  7.2 51.1 %all-gather.3.cloned.1.call-start = ((), (), s32[]{:S(2)}) async-start(), calls=%async_computation.2 | async-start | bytes 2621440 | tf_op jit(solution)/shard_map/all_gather | solution.py:19
  7.9 96.6 %all-gather.5.cloned.1.call-start = ((), (), s32[]{:S(2)}) async-start(), calls=%async_computation.3 | async-start | bytes 2621440 | tf_op jit(solution)/shard_map/all_gather | solution.py:20
  8.6 732.7 %reduce-scatter.5.cloned.1.call-start = ((), (), s32[]{:S(2)}) async-start(), calls=%async_computation.5 | async-start | bytes 5242880 | tf_op jit(solution)/shard_map/reduce_scatter | solution.py:129
  58.2 48.3 %copy-start = (bf16[1,4,512,512]{3,2,1,0:T(8,128)(2,1)S(1)}, bf16[1,4,512,512]{3,2,1,0:T(8,128)(2,1)}, u32[]{:S(2)}) copy-start(bf16[1,4,512,512]{3,2,1,0:T(8,128)(2,1)} %all-gather.3.cloned.1.call-done) | copy-start | bytes 6291460
  114.5 3.1 collective-permute-start
  125.5 3.1 collective-permute-start
  136.5 3.7 collective-permute-start
  148.2 5.6 collective-permute-start
  161.8 5.5 collective-permute-start
  175.3 5.6 collective-permute-start
  188.8 5.6 collective-permute-start
  202.4 5.6 collective-permute-start
  215.9 5.6 collective-permute-start
  229.5 5.6 collective-permute-start
  243.0 5.6 collective-permute-start
  256.5 5.6 collective-permute-start
  263.4 12.2 %collective-permute-start = (bf16[64,512]{1,0:T(8,128)(2,1)S(1)}, bf16[64,512]{1,0:T(8,128)(2,1)S(1)}, u32[]{:S(2)}, u32[]{:S(2)}) collective-permute-start(bf16[64,512]{1,0:T(8,128)(2,1)S(1)} %get-tuple-element.520), channel_id=1, source_target_pairs={{0,4},{4,8},{8,12},{12,16},{16,20},{20,24},{24,28},{1,5},{5,9},{9,... | collective-permute-start | bytes 196616 | tf_op jit(solution)/shard_map/while/body/eval_jaxpr/ppermute | solution.py:11
  277.0 5.6 collective-permute-start
  283.9 13.1 %collective-permute-start = (bf16[64,512]{1,0:T(8,128)(2,1)S(1)}, bf16[64,512]{1,0:T(8,128)(2,1)S(1)}, u32[]{:S(2)}, u32[]{:S(2)}) collective-permute-start(bf16[64,512]{1,0:T(8,128)(2,1)S(1)} %get-tuple-element.520), channel_id=1, source_target_pairs={{0,4},{4,8},{8,12},{12,16},{16,20},{20,24},{24,28},{1,5},{5,9},{9,... | collective-permute-start | bytes 196616 | tf_op jit(solution)/shard_map/while/body/eval_jaxpr/ppermute | solution.py:11
  298.4 6.5 collective-permute-start
  306.2 13.1 %collective-permute-start = (bf16[64,512]{1,0:T(8,128)(2,1)S(1)}, bf16[64,512]{1,0:T(8,128)(2,1)S(1)}, u32[]{:S(2)}, u32[]{:S(2)}) collective-permute-start(bf16[64,512]{1,0:T(8,128)(2,1)S(1)} %get-tuple-element.520), channel_id=1, source_target_pairs={{0,4},{4,8},{8,12},{12,16},{16,20},{20,24},{24,28},{1,5},{5,9},{9,... | collective-permute-start | bytes 196616 | tf_op jit(solution)/shard_map/while/body/eval_jaxpr/ppermute | solution.py:11
  320.6 6.5 collective-permute-start
  328.5 13.1 %collective-permute-start = (bf16[64,512]{1,0:T(8,128)(2,1)S(1)}, bf16[64,512]{1,0:T(8,128)(2,1)S(1)}, u32[]{:S(2)}, u32[]{:S(2)}) collective-permute-start(bf16[64,512]{1,0:T(8,128)(2,1)S(1)} %get-tuple-element.520), channel_id=1, source_target_pairs={{0,4},{4,8},{8,12},{12,16},{16,20},{20,24},{24,28},{1,5},{5,9},{9,... | collective-permute-start | bytes 196616 | tf_op jit(solution)/shard_map/while/body/eval_jaxpr/ppermute | solution.py:11
  349.2 5.9 collective-permute-start.1
  356.5 6.7 collective-permute-start.1
  364.5 6.6 collective-permute-start.1
  372.4 8.5 %collective-permute-start.1 = (bf16[64,512]{1,0:T(8,128)(2,1)S(1)}, bf16[64,512]{1,0:T(8,128)(2,1)S(1)}, u32[]{:S(2)}, u32[]{:S(2)}) collective-permute-start(bf16[64,512]{1,0:T(8,128)(2,1)S(1)} %get-tuple-element.534), channel_id=1, source_target_pairs={{4,0},{8,4},{12,8},{16,12},{20,16},{24,20},{28,24},{5,1},{9,5},{13... | collective-permute-start | bytes 196616 | tf_op jit(solution)/shard_map/while/body/eval_jaxpr/ppermute | solution.py:11
  382.3 6.6 collective-permute-start.1
  390.2 6.6 collective-permute-start.1
  398.1 62.2 %collective-permute-start.1 = (bf16[64,512]{1,0:T(8,128)(2,1)S(1)}, bf16[64,512]{1,0:T(8,128)(2,1)S(1)}, u32[]{:S(2)}, u32[]{:S(2)}) collective-permute-start(bf16[64,512]{1,0:T(8,128)(2,1)S(1)} %get-tuple-element.534), channel_id=1, source_target_pairs={{4,0},{8,4},{12,8},{16,12},{20,16},{24,20},{28,24},{5,1},{9,5},{13... | collective-permute-start | bytes 196616 | tf_op jit(solution)/shard_map/while/body/eval_jaxpr/ppermute | solution.py:11
  470.4 6.6 collective-permute-start.1
  478.2 6.9 copy-start.4
  487.1 6.6 collective-permute-start.1
  495.0 6.9 copy-start.4
  503.8 6.6 collective-permute-start.1
  520.5 6.6 collective-permute-start.1
  528.3 6.9 copy-start.4
  537.2 6.6 collective-permute-start.1
  553.9 6.6 collective-permute-start.1
  570.6 6.6 collective-permute-start.1
  587.3 6.6 collective-permute-start.1
  604.0 6.6 collective-permute-start.1
  620.7 6.6 collective-permute-start.1
  637.4 6.6 collective-permute-start.1
  654.1 6.0 collective-permute-start.1
  666.7 154.1 %reduce-scatter.3.cloned.1.call-start = ((), (), s32[]{:S(2)}) async-start(), calls=%async_computation.4 | async-start | bytes 5242880 | tf_op jit(solution)/shard_map/reduce_scatter | solution.py:128
  674.4 67.0 %copy-start.2 = (bf16[1,4,128,512]{3,2,1,0:T(8,128)(2,1)S(1)}, bf16[1,4,128,512]{3,2,1,0:T(8,128)(2,1)}, u32[]{:S(2)}) copy-start(bf16[1,4,128,512]{3,2,1,0:T(8,128)(2,1)} %param.15) | copy-start | bytes 1572868
  674.4 146.5 %copy-start.3 = (bf16[1,4,128,512]{3,2,1,0:T(8,128)(2,1)S(1)}, bf16[1,4,128,512]{3,2,1,0:T(8,128)(2,1)}, u32[]{:S(2)}) copy-start(bf16[1,4,128,512]{3,2,1,0:T(8,128)(2,1)} %param.14) | copy-start | bytes 1572868
  (10 other events, 64.2 us)
Sparse Core Ops, SparseCore 0:
  9.6 48.6 all-gather.2
  59.8 44.6 all-gather.4
  666.9 74.4 reduce-scatter.4
  743.6 77.2 reduce-scatter.2
where the time goes:
time: 839 us; the launch traced here: 830 us
  waiting for transfers between devices  310 us (37%)
  matrix products  171 us (20%)
  starting transfers between devices  121 us (14%)
  local copies, waits for them, and re-layouts  108 us (13%)
  other arithmetic  77.8 us (9%)
  loops' own time  27.8 us (3%)
  between operations  13.8 us (2%)
    ppermute x38, starting transfers between devices, shifted(): lax.ppermute(value, axis, [(source, source + steps) for source in range(i...  121 us
    reduce_scatter x1, waiting for transfers between devices, per_device(): lax.psum_scatter(grad_in, 'dp', scatter_dimension=1, tiled=True)  77.2 us
    dynamic_slice x76, local copies, waits for them, and re-layouts, put(): old = lax.dynamic_index_in_dim(store, index, axis_pos, keepdims=False)  74.4 us
    dot_general x48, matrix products, forward_section(): jnp.dot(hidden, second[layer], preferred_element_type=jnp.float32)  68.7 us
    ppermute x38, waiting for transfers between devices, shifted(): lax.ppermute(value, axis, [(source, source + steps) for source in range(i...  68.3 us
    reduce_scatter x1, waiting for transfers between devices, per_device(): lax.psum_scatter(grad_out, 'dp', scatter_dimension=1, tiled=True)  66.9 us
    dot_general x48, matrix products, backward_section(): pre = jnp.dot(value, first[layer], preferred_element_type=jnp.float32)  50.1 us
    all_gather x1, waiting for transfers between devices, per_device(): lax.all_gather(w_in, 'dp', axis=2, tiled=True)  49.5 us
  transfers between devices with their start and end apart: 42, of which 21 were waited for; matrix products, arithmetic and copies ran while one was open for 16% of the time, Pallas kernels for 0%

commit v1 on v0

--- a/solution.py
+++ b/solution.py
@@ -3,6 +3,27 @@
 import jax.numpy as jnp
 from jax import lax
 from jax.sharding import PartitionSpec as P
+
+
+def ring_gather(shard, axis, dim):
+    count, index, extent = (lax.axis_size(axis), lax.axis_index(axis), shard.shape[dim])
+    right = [(i, (i + 1) % count) for i in range(count)]
+    left = [(i, (i - 1) % count) for i in range(count)]
+    out = jnp.zeros((*shard.shape[:dim], count * extent, *shard.shape[dim + 1 :]), shard.dtype)
+    out = lax.dynamic_update_slice_in_dim(out, shard, index * extent, axis=dim)
+    from_left = from_right = shard
+    halfway = count // 2
+    for hop in range(1, halfway + 1):
+        from_left = lax.ppermute(from_left, axis, right)
+        out = lax.dynamic_update_slice_in_dim(
+            out, from_left, (index - hop) % count * extent, axis=dim
+        )
+        if hop < count - halfway:
+            from_right = lax.ppermute(from_right, axis, left)
+            out = lax.dynamic_update_slice_in_dim(
+                out, from_right, (index + hop) % count * extent, axis=dim
+            )
+    return out
 
 
 def shifted(value, axis, steps):
@@ -17,7 +38,7 @@
     groups = lax.axis_size("dp")
     full_in, full_out = (
         lax.all_gather(w_in, "dp", axis=2, tiled=True),
-        lax.all_gather(w_out, "dp", axis=2, tiled=True),
+        ring_gather(w_out, "dp", 2),
     )
     first = full_in[0]
     second = full_out[0]

time: 839 us -> 797 us (0.950)
  waiting for transfers between devices: 310 us -> 266 us
  matrix products: 171 us -> 159 us
  starting transfers between devices: 121 us -> 132 us
    ppermute x0 -> x3, waiting for transfers between devices: none -> 51.4 us  [the longest x1 33.6 us: ring_gather(): from_right = lax.ppermute(from_right, axis, left)]
    all_gather x1 -> x0, waiting for transfers between devices: 46.3 us -> none  [per_device(): lax.all_gather(w_out, 'dp', axis=2, tiled=True)]
    all_gather x1, waiting for transfers between devices: 49.5 us -> 7.71 us  [per_device(): lax.all_gather(w_in, 'dp', axis=2, tiled=True)]
    dot_general x48, matrix products: 26.2 us -> 13.7 us  [backward_section(): lax.dot_general(grad, second[layer], contract, preferred_element_type=jnp...]
    ppermute x0 -> x3, starting transfers between devices: none -> 10.9 us  [the longest x2 8.8 us: ring_gather(): from_left = lax.ppermute(from_left, axis, right)]
  transfers between devices with their start and end apart: 42 -> 44, of which waited for: 21 -> 23; matrix products, arithmetic and copies ran while one was open for 16% -> 17% of each run, Pallas kernels for 0% -> 0%
where the time goes in v1:
time: 797 us; the launch traced here: 788 us
  waiting for transfers between devices  266 us (33%)
  matrix products  159 us (20%)
  starting transfers between devices  132 us (17%)
  local copies, waits for them, and re-layouts  112 us (14%)
  other arithmetic  78 us (10%)
  loops' own time  28 us (4%)
  between operations  13.9 us (2%)
    ppermute x38, starting transfers between devices, shifted(): lax.ppermute(value, axis, [(source, source + steps) for source in range(i...  121 us
    reduce_scatter x1, waiting for transfers between devices, per_device(): lax.psum_scatter(grad_in, 'dp', scatter_dimension=1, tiled=True)  77.3 us
    dynamic_slice x76, local copies, waits for them, and re-layouts, put(): old = lax.dynamic_index_in_dim(store, index, axis_pos, keepdims=False)  74.4 us
    dot_general x48, matrix products, forward_section(): jnp.dot(hidden, second[layer], preferred_element_type=jnp.float32)  68.8 us
    reduce_scatter x1, waiting for transfers between devices, per_device(): lax.psum_scatter(grad_out, 'dp', scatter_dimension=1, tiled=True)  67.5 us
    ppermute x38, waiting for transfers between devices, shifted(): lax.ppermute(value, axis, [(source, source + steps) for source in range(i...  60.9 us
    dot_general x48, matrix products, backward_section(): pre = jnp.dot(value, first[layer], preferred_element_type=jnp.float32)  50.1 us
    dynamic_update_slice x57, other arithmetic, put(): lax.dynamic_update_index_in_dim(store, jnp.where(valid, fresh, old), inde...  47.4 us
  transfers between devices with their start and end apart: 44, of which 23 were waited for; matrix products, arithmetic and copies ran while one was open for 17% of the time, Pallas kernels for 0%

profile of v1, /device:TPU:0, one launch (start us, length us, event | category | flops | bytes accessed | tf_op | source)
XLA Modules:
  0.0 787.9 jit_solution(17002235629283395439)
XLA Ops:
  13.1 14.3 %collective-permute-done.2 = bf16[1,4,128,512]{3,2,1,0:T(8,128)(2,1)S(1)} collective-permute-done((bf16[1,4,128,512]{3,2,1,0:T(8,128)(2,1)}, bf16[1,4,128,512]{3,2,1,0:T(8,128)(2,1)S(1)}, u32[]{:S(2)}, u32[]{:S(2)}) %collective-permute-start.2) | collective-permute-done | bytes 524320 | tf_op jit(solution)/shard_map/ppermute | solution.py:17
  27.4 5.7 collective-permute-start.4
  33.5 33.6 %collective-permute-done.3 = bf16[1,4,128,512]{3,2,1,0:T(8,128)(2,1)} collective-permute-done((bf16[1,4,128,512]{3,2,1,0:T(8,128)(2,1)}, bf16[1,4,128,512]{3,2,1,0:T(8,128)(2,1)}, u32[]{:S(2)}, u32[]{:S(2)}) %collective-permute-start.3) | collective-permute-done | bytes 524320 | tf_op jit(solution)/shard_map/ppermute | solution.py:22
  74.1 7.7 all-gather.2.cloned.1.call-done
  84.0 234.7 %while.31 = (s32[]{:T(128)}, bf16[64,512]{1,0:T(8,128)(2,1)S(1)}, bf16[4,12,64,512]{3,2,1,0:T(8,128)(2,1)}, s32[19]{0:T(128)S(1)}, s32[]{:T(128)}, /*index=5*/pr...) while((s32[]{:T(128)}, bf16[64,512]{1,0:T(8,128)(2,1)S(1)}, ...), condition=%wide.region_3.4_spmd, body=%wide.region_0.3_spmd.sunk | while | flops 270106624 | bytes 7408441 | solution.py:103
  85.2 6.7 conditional.4
  96.2 6.7 conditional.4
  107.3 6.7 conditional.4
  118.9 6.7 conditional.4
  125.6 3.8 collective-permute-start
  132.4 6.7 conditional.4
  145.9 6.7 conditional.4
  152.6 3.8 collective-permute-start
  159.5 6.7 conditional.4
  166.1 3.8 collective-permute-start
  173.0 6.7 conditional.4
  186.5 6.7 conditional.4
  193.2 3.9 collective-permute-start
  200.0 6.7 conditional.4
  206.7 3.8 collective-permute-start
  213.6 6.7 conditional.4
  220.2 3.8 collective-permute-start
  227.1 6.7 conditional.4
  240.6 10.5 %collective-permute-start = (bf16[64,512]{1,0:T(8,128)(2,1)S(1)}, bf16[64,512]{1,0:T(8,128)(2,1)S(1)}, u32[]{:S(2)}, u32[]{:S(2)}) collective-permute-start(bf16[64,512]{1,0:T(8,128)(2,1)S(1)} %get-tuple-element.520), channel_id=1, source_target_pairs={{0,4},{4,8},{8,12},{12,16},{16,20},{20,24},{24,28},{1,5},{5,9},{9,... | collective-permute-start | bytes 196616 | tf_op jit(solution)/shard_map/while/body/eval_jaxpr/ppermute | solution.py:32
  254.1 3.9 collective-permute-start
  261.2 11.3 %collective-permute-start = (bf16[64,512]{1,0:T(8,128)(2,1)S(1)}, bf16[64,512]{1,0:T(8,128)(2,1)S(1)}, u32[]{:S(2)}, u32[]{:S(2)}) collective-permute-start(bf16[64,512]{1,0:T(8,128)(2,1)S(1)} %get-tuple-element.520), channel_id=1, source_target_pairs={{0,4},{4,8},{8,12},{12,16},{16,20},{20,24},{24,28},{1,5},{5,9},{9,... | collective-permute-start | bytes 196616 | tf_op jit(solution)/shard_map/while/body/eval_jaxpr/ppermute | solution.py:32
  275.6 4.7 collective-permute-start
  283.4 11.4 %collective-permute-start = (bf16[64,512]{1,0:T(8,128)(2,1)S(1)}, bf16[64,512]{1,0:T(8,128)(2,1)S(1)}, u32[]{:S(2)}, u32[]{:S(2)}) collective-permute-start(bf16[64,512]{1,0:T(8,128)(2,1)S(1)} %get-tuple-element.520), channel_id=1, source_target_pairs={{0,4},{4,8},{8,12},{12,16},{16,20},{20,24},{24,28},{1,5},{5,9},{9,... | collective-permute-start | bytes 196616 | tf_op jit(solution)/shard_map/while/body/eval_jaxpr/ppermute | solution.py:32
  297.8 4.7 collective-permute-start
  305.6 11.3 %collective-permute-start = (bf16[64,512]{1,0:T(8,128)(2,1)S(1)}, bf16[64,512]{1,0:T(8,128)(2,1)S(1)}, u32[]{:S(2)}, u32[]{:S(2)}) collective-permute-start(bf16[64,512]{1,0:T(8,128)(2,1)S(1)} %get-tuple-element.520), channel_id=1, source_target_pairs={{0,4},{4,8},{8,12},{12,16},{16,20},{20,24},{24,28},{1,5},{5,9},{9,... | collective-permute-start | bytes 196616 | tf_op jit(solution)/shard_map/while/body/eval_jaxpr/ppermute | solution.py:32
  324.9 292.5 %while.32 = (s32[]{:T(128)}, bf16[64,512]{1,0:T(8,128)(2,1)S(1)}, bf16[4,12,64,512]{3,2,1,0:T(8,128)(2,1)}, bf16[4,12,64,512]{3,2,1,0:T(8,128)(2,1)}, bf16[4,12,...) while((s32[]{:T(128)}, bf16[64,512]{1,0:T(8,128)(2,1)S(1)}, ...), condition=%wide.region_7.8_spmd, body=%wide.region_4.7_spmd.sunk | while | flops 406487040 | bytes 24055228 | solution.py:135
  381.2 48.9 %collective-permute-done.1 = bf16[64,512]{1,0:T(8,128)(2,1)S(1)} collective-permute-done((bf16[64,512]{1,0:T(8,128)(2,1)S(1)}, bf16[64,512]{1,0:T(8,128)(2,1)S(1)}, u32[]{:S(2)}, u32[]{:S(2)}) %collective-permute-start.1) | collective-permute-done | bytes 65568 | tf_op jit(solution)/shard_map/while/body/eval_jaxpr/ppermute | solution.py:32
  431.4 7.8 conditional.5
  447.0 7.8 conditional.5
  462.7 7.8 conditional.5
  478.3 7.8 conditional.5
  494.0 7.8 conditional.5
  509.7 7.8 conditional.5
  525.4 7.8 conditional.5
  541.0 7.8 conditional.5
  556.7 7.8 conditional.5
  572.3 7.8 conditional.5
  588.0 7.8 conditional.5
  603.7 7.8 conditional.5
  617.4 6.6 fusion.96
  626.0 5.7 fusion.95
  631.7 67.5 %reduce-scatter.5.cloned.1.call-done = f32[4,128,512]{2,1,0:T(8,128)} async-done(((f32[4,512,512]{2,1,0:T(8,128)}), f32[4,128,512]{2,1,0:T(8,128)}) %reduce-scatter.5.cloned.1.call-update) | async-done | bytes 1048592 | tf_op jit(solution)/shard_map/reduce_scatter | solution.py:150
  701.6 77.3 %reduce-scatter.3.cloned.1.call-done = f32[4,128,512]{2,1,0:T(8,128)} async-done(((f32[4,512,512]{2,1,0:T(8,128)}), f32[4,128,512]{2,1,0:T(8,128)}) %reduce-scatter.3.cloned.1.call-update) | async-done | bytes 1048592 | tf_op jit(solution)/shard_map/reduce_scatter | solution.py:149
  (625 shorter events, 399.0 us)
Async XLA Ops:
  7.2 26.2 %copy-start.5 = (bf16[1,4,128,512]{3,2,1,0:T(8,128)(2,1)S(1)}, bf16[1,4,128,512]{3,2,1,0:T(8,128)(2,1)}, u32[]{:S(2)}) copy-start(bf16[1,4,128,512]{3,2,1,0:T(8,128)(2,1)} %param.15) | copy-start | bytes 1572868
  7.2 74.6 %all-gather.2.cloned.1.call-start = ((), (), s32[]{:S(2)}) async-start(), calls=%async_computation.2 | async-start | bytes 2621440 | tf_op jit(solution)/shard_map/all_gather | solution.py:40
  7.9 691.3 %reduce-scatter.5.cloned.1.call-start = ((), (), s32[]{:S(2)}) async-start(), calls=%async_computation.4 | async-start | bytes 5242880 | tf_op jit(solution)/shard_map/reduce_scatter | solution.py:150
  8.0 19.5 %collective-permute-start.2 = (bf16[1,4,128,512]{3,2,1,0:T(8,128)(2,1)}, bf16[1,4,128,512]{3,2,1,0:T(8,128)(2,1)S(1)}, u32[]{:S(2)}, u32[]{:S(2)}) collective-permute-start(bf16[1,4,128,512]{3,2,1,0:T(8,128)(2,1)} %param.15), channel_id=1, source_target_pairs={{0,1},{1,2},{2,3},{3,0},{4,5},{5,6},{6,7},{7,4},{8,9},{9,10},{10,1... | collective-permute-start | bytes 1572872 | tf_op jit(solution)/shard_map/ppermute | solution.py:17
  11.0 56.1 %collective-permute-start.3 = (bf16[1,4,128,512]{3,2,1,0:T(8,128)(2,1)}, bf16[1,4,128,512]{3,2,1,0:T(8,128)(2,1)}, u32[]{:S(2)}, u32[]{:S(2)}) collective-permute-start(bf16[1,4,128,512]{3,2,1,0:T(8,128)(2,1)} %param.15), channel_id=1, source_target_pairs={{0,3},{1,0},{2,1},{3,2},{4,7},{5,4},{6,5},{7,6},{8,11},{9,8},{10,9... | collective-permute-start | bytes 1572872 | tf_op jit(solution)/shard_map/ppermute | solution.py:22
  27.4 44.2 %collective-permute-start.4 = (bf16[1,4,128,512]{3,2,1,0:T(8,128)(2,1)S(1)}, bf16[1,4,128,512]{3,2,1,0:T(8,128)(2,1)}, u32[]{:S(2)}, u32[]{:S(2)}) collective-permute-start(bf16[1,4,128,512]{3,2,1,0:T(8,128)(2,1)S(1)} %collective-permute-done.2), channel_id=1, source_target_pairs={{0,1},{1,2},{2,3},{3,0},{4,5},{5,6},{6,7},{7,4},{8,9},{9,10},{10,1... | collective-permute-start | bytes 1572872 | tf_op jit(solution)/shard_map/ppermute | solution.py:17
  91.9 3.1 collective-permute-start
  102.9 3.1 collective-permute-start
  114.0 3.7 collective-permute-start
  125.6 5.6 collective-permute-start
  139.1 5.5 collective-permute-start
  152.6 5.6 collective-permute-start
  166.1 5.6 collective-permute-start
  179.7 5.6 collective-permute-start
  193.2 5.6 collective-permute-start
  206.7 5.6 collective-permute-start
  220.2 5.6 collective-permute-start
  233.7 5.6 collective-permute-start
  240.6 12.2 %collective-permute-start = (bf16[64,512]{1,0:T(8,128)(2,1)S(1)}, bf16[64,512]{1,0:T(8,128)(2,1)S(1)}, u32[]{:S(2)}, u32[]{:S(2)}) collective-permute-start(bf16[64,512]{1,0:T(8,128)(2,1)S(1)} %get-tuple-element.520), channel_id=1, source_target_pairs={{0,4},{4,8},{8,12},{12,16},{16,20},{20,24},{24,28},{1,5},{5,9},{9,... | collective-permute-start | bytes 196616 | tf_op jit(solution)/shard_map/while/body/eval_jaxpr/ppermute | solution.py:32
  254.1 5.7 collective-permute-start
  261.2 13.1 %collective-permute-start = (bf16[64,512]{1,0:T(8,128)(2,1)S(1)}, bf16[64,512]{1,0:T(8,128)(2,1)S(1)}, u32[]{:S(2)}, u32[]{:S(2)}) collective-permute-start(bf16[64,512]{1,0:T(8,128)(2,1)S(1)} %get-tuple-element.520), channel_id=1, source_target_pairs={{0,4},{4,8},{8,12},{12,16},{16,20},{20,24},{24,28},{1,5},{5,9},{9,... | collective-permute-start | bytes 196616 | tf_op jit(solution)/shard_map/while/body/eval_jaxpr/ppermute | solution.py:32
  275.6 6.5 collective-permute-start
  283.4 13.1 %collective-permute-start = (bf16[64,512]{1,0:T(8,128)(2,1)S(1)}, bf16[64,512]{1,0:T(8,128)(2,1)S(1)}, u32[]{:S(2)}, u32[]{:S(2)}) collective-permute-start(bf16[64,512]{1,0:T(8,128)(2,1)S(1)} %get-tuple-element.520), channel_id=1, source_target_pairs={{0,4},{4,8},{8,12},{12,16},{16,20},{20,24},{24,28},{1,5},{5,9},{9,... | collective-permute-start | bytes 196616 | tf_op jit(solution)/shard_map/while/body/eval_jaxpr/ppermute | solution.py:32
  297.8 6.5 collective-permute-start
  305.6 13.1 %collective-permute-start = (bf16[64,512]{1,0:T(8,128)(2,1)S(1)}, bf16[64,512]{1,0:T(8,128)(2,1)S(1)}, u32[]{:S(2)}, u32[]{:S(2)}) collective-permute-start(bf16[64,512]{1,0:T(8,128)(2,1)S(1)} %get-tuple-element.520), channel_id=1, source_target_pairs={{0,4},{4,8},{8,12},{12,16},{16,20},{20,24},{24,28},{1,5},{5,9},{9,... | collective-permute-start | bytes 196616 | tf_op jit(solution)/shard_map/while/body/eval_jaxpr/ppermute | solution.py:32
  326.3 6.0 collective-permute-start.1
  333.6 6.6 collective-permute-start.1
  341.6 6.6 collective-permute-start.1
  349.6 8.4 %collective-permute-start.1 = (bf16[64,512]{1,0:T(8,128)(2,1)S(1)}, bf16[64,512]{1,0:T(8,128)(2,1)S(1)}, u32[]{:S(2)}, u32[]{:S(2)}) collective-permute-start(bf16[64,512]{1,0:T(8,128)(2,1)S(1)} %get-tuple-element.534), channel_id=1, source_target_pairs={{4,0},{8,4},{12,8},{16,12},{20,16},{24,20},{28,24},{5,1},{9,5},{13... | collective-permute-start | bytes 196616 | tf_op jit(solution)/shard_map/while/body/eval_jaxpr/ppermute | solution.py:32
  359.4 6.6 collective-permute-start.1
  367.3 6.6 collective-permute-start.1
  375.3 54.8 %collective-permute-start.1 = (bf16[64,512]{1,0:T(8,128)(2,1)S(1)}, bf16[64,512]{1,0:T(8,128)(2,1)S(1)}, u32[]{:S(2)}, u32[]{:S(2)}) collective-permute-start(bf16[64,512]{1,0:T(8,128)(2,1)S(1)} %get-tuple-element.534), channel_id=1, source_target_pairs={{4,0},{8,4},{12,8},{16,12},{20,16},{24,20},{28,24},{5,1},{9,5},{13... | collective-permute-start | bytes 196616 | tf_op jit(solution)/shard_map/while/body/eval_jaxpr/ppermute | solution.py:32
  439.2 6.6 collective-permute-start.1
  454.8 6.6 collective-permute-start.1
  470.5 6.6 collective-permute-start.1
  486.2 6.6 collective-permute-start.1
  494.0 5.2 copy-start.4
  501.8 6.6 collective-permute-start.1
  517.5 6.6 collective-permute-start.1
  533.2 6.6 collective-permute-start.1
  548.9 6.6 collective-permute-start.1
  564.5 6.6 collective-permute-start.1
  580.2 6.6 collective-permute-start.1
  595.8 6.6 collective-permute-start.1
  611.5 6.0 collective-permute-start.1
  624.1 154.9 %reduce-scatter.3.cloned.1.call-start = ((), (), s32[]{:S(2)}) async-start(), calls=%async_computation.3 | async-start | bytes 5242880 | tf_op jit(solution)/shard_map/reduce_scatter | solution.py:149
  631.7 67.6 %copy-start.6 = (bf16[1,4,128,512]{3,2,1,0:T(8,128)(2,1)S(1)}, bf16[1,4,128,512]{3,2,1,0:T(8,128)(2,1)}, u32[]{:S(2)}) copy-start(bf16[1,4,128,512]{3,2,1,0:T(8,128)(2,1)} %param.15) | copy-start | bytes 1572868
  631.7 147.3 %copy-start.2 = (bf16[1,4,128,512]{3,2,1,0:T(8,128)(2,1)S(1)}, bf16[1,4,128,512]{3,2,1,0:T(8,128)(2,1)}, u32[]{:S(2)}) copy-start(bf16[1,4,128,512]{3,2,1,0:T(8,128)(2,1)} %param.14) | copy-start | bytes 1572868
  (14 other events, 62.8 us)
Sparse Core Ops, SparseCore 0:
  9.6 72.1 all-gather.1
  624.2 74.9 reduce-scatter.4
  701.7 77.2 reduce-scatter.2
